TPU v7x, 32 devices: a whole 2x2x4 slice. The times are simulated.
32 devices in a mesh: expert: 16 (over z, y, x), dp: 2 (over core).
Axes of the slice: x: 2, y: 2, z: 4, core: 2. Of those that a mesh axis runs over, the one named last changes fastest.
Arguments:
- layer_input: bfloat16 [4096, 3584], P(('expert', 'dp')), may hold values from -6 to 6
- out_grad: bfloat16 [4096, 3584], P(('expert', 'dp')), may hold values from -6 to 6
- routes: int32 [4096, 8], P(('expert', 'dp')), may hold values from 0 to 255, as said below
- gate_values: float32 [4096, 8], P(('expert', 'dp')), may hold values from 0.1 to 1
- keep_mask: int32 [4096, 8], P(('expert', 'dp')), may hold values 0 or 1
- gate_weight: bfloat16 [3584, 6144], P('dp', 'expert'), may hold values from -0.09375 to 0.09375
- up_weight: bfloat16 [3584, 6144], P('dp', 'expert'), may hold values from -0.09375 to 0.09375
- down_transposed: bfloat16 [3584, 6144], P('dp', 'expert'), may hold values from -0.15625 to 0.15625
Outputs:
- input_grad: bfloat16 [4096, 3584], P(('expert', 'dp'))
- gate_grad: bfloat16 [3584, 6144], P('dp', 'expert')
- up_grad: bfloat16 [3584, 6144], P('dp', 'expert')
- down_grad: bfloat16 [3584, 6144], P('dp', 'expert')
Inputs may be any that keep to these rules, and one draw needn't show every extreme that they name: `routes`: each token names 8 different experts. Among one device's 128 tokens no expert is named more than 5 times; on every device some expert below 4 is named exactly 5 times, and one expert below 4 is named 5 times on every device.
All inputs are finite; a program needn't handle non-finite values. No bound on the sum of `keep_mask` on one device may be relied on, other than what follows from the above.
Results may differ from a plain program's by a relative error of at most 0.0065.
Values may be sent and summed in bfloat16 or wider, within the bound.
No kernel may reach another device: no remote copies, remote signals or barrier semaphores. Data moves between devices by JAX's collectives and lax.ppermute only.
A program may use at most 128 MiB of HBM per device.

v0:
```python
import jax
import jax.numpy as jnp
from jax import lax
from jax.sharding import PartitionSpec as P

TOP = 8
SPLIT = 4
MOST = 5


def as_sent(array):
    return jax.tree.map(lambda a: a.astype(jnp.bfloat16) if a.dtype == jnp.float32 else a, array)


def silu_parts(pre_gate):
    sigma = jax.nn.sigmoid(pre_gate)
    return (pre_gate * sigma, sigma * (1.0 + pre_gate * (1.0 - sigma)))


def route_tables(routes, keep_mask, live_count, slot_count):
    flat_routes = routes.reshape(-1)
    flat_keep = keep_mask.reshape(-1)
    expert_iota = jnp.arange(live_count, dtype=jnp.int32)
    chosen = ((flat_routes[:, None] == expert_iota[None, :]) & (flat_keep[:, None] == 1)).astype(
        jnp.int32
    )
    route_ranks = jnp.cumsum(chosen, axis=0) - 1
    slot_iota = jnp.arange(slot_count, dtype=jnp.int32)
    matched = chosen[:, :, None] * (route_ranks[:, :, None] == slot_iota[None, None, :]).astype(
        jnp.int32
    )
    route_iota = jnp.arange(flat_routes.shape[0], dtype=jnp.int32)
    picked = jnp.sum(matched * route_iota[:, None, None], axis=0)
    filled = jnp.sum(matched, axis=0)
    return (picked.reshape(-1), filled.reshape(-1))


def expert_backward(slot_inputs, slot_grads, weights):
    gate_full, up_full, down_full = weights
    pre_gate = jnp.dot(slot_inputs, gate_full, preferred_element_type=jnp.float32)
    pre_up = jnp.dot(slot_inputs, up_full, preferred_element_type=jnp.float32)
    activated, slope = silu_parts(pre_gate)
    hidden = (activated * pre_up).astype(jnp.bfloat16)
    hidden_grad = jnp.dot(slot_grads, down_full, preferred_element_type=jnp.float32)
    gate_side = (hidden_grad * pre_up * slope).astype(jnp.bfloat16)
    up_side = (hidden_grad * activated).astype(jnp.bfloat16)
    across = (((1,), (1,)), ((), ()))
    partial_value = lax.dot_general(
        gate_side, gate_full, across, preferred_element_type=jnp.float32
    )
    partial_value = partial_value + lax.dot_general(
        up_side, up_full, across, preferred_element_type=jnp.float32
    )
    rows_first = (((0,), (0,)), ((), ()))
    weight_terms = (
        lax.dot_general(slot_inputs, gate_side, rows_first, preferred_element_type=jnp.float32),
        lax.dot_general(slot_inputs, up_side, rows_first, preferred_element_type=jnp.float32),
        lax.dot_general(slot_grads, hidden, rows_first, preferred_element_type=jnp.float32),
    )
    return (partial_value.astype(jnp.bfloat16), weight_terms)


def body(
    layer_input, out_grad, routes, gate_values, keep_mask, gate_weight, up_weight, down_transposed
):
    devices = lax.axis_size("expert")
    live_count = devices // SPLIT
    token_count = layer_input.shape[0]
    model_width = layer_input.shape[1]
    weights = (
        lax.all_gather(gate_weight, "dp", axis=0, tiled=True),
        lax.all_gather(up_weight, "dp", axis=0, tiled=True),
        lax.all_gather(down_transposed, "dp", axis=0, tiled=True),
    )
    slot_count = MOST
    picked, filled = route_tables(routes, keep_mask, live_count, slot_count)
    token_of = picked // TOP
    route_scale = jnp.take(gate_values.reshape(-1), picked) * filled.astype(jnp.float32)
    sent_inputs = (
        jnp.take(layer_input, token_of, axis=0) * filled.astype(layer_input.dtype)[:, None]
    )
    sent_grads = (
        jnp.take(out_grad, token_of, axis=0).astype(jnp.float32) * route_scale[:, None]
    ).astype(jnp.bfloat16)
    expanded = (live_count, SPLIT, MOST, model_width)
    copies_in = jnp.broadcast_to(
        sent_inputs.reshape(live_count, 1, MOST, model_width), expanded
    ).reshape(-1, model_width)
    copies_grad = jnp.broadcast_to(
        sent_grads.reshape(live_count, 1, MOST, model_width), expanded
    ).reshape(-1, model_width)
    slot_inputs, slot_grads = (
        lax.all_to_all(copies_in, "expert", split_axis=0, concat_axis=0, tiled=True),
        lax.all_to_all(copies_grad, "expert", split_axis=0, concat_axis=0, tiled=True),
    )
    partial_value, weight_terms = expert_backward(slot_inputs, slot_grads, weights)
    returned = lax.all_to_all(partial_value, "expert", split_axis=0, concat_axis=0, tiled=True)
    summed = jnp.sum(
        returned.reshape(live_count, SPLIT, MOST, model_width).astype(jnp.float32), axis=1
    )
    summed = summed.reshape(-1, model_width)
    table_tokens = token_of.reshape(live_count, slot_count).reshape(-1)
    table_live = filled.reshape(live_count, slot_count).reshape(-1)
    token_iota = jnp.arange(token_count, dtype=jnp.int32)
    placing = ((token_iota[:, None] == table_tokens[None, :]) & (table_live[None, :] == 1)).astype(
        jnp.float32
    )
    input_grad = jnp.dot(
        placing, summed, precision=lax.Precision.HIGHEST, preferred_element_type=jnp.float32
    ).astype(jnp.bfloat16)
    rounded = tuple(
        (
            lax.optimization_barrier(weight_term.astype(jnp.bfloat16)).astype(jnp.float32)
            for weight_term in weight_terms
        )
    )
    gate_grad, up_grad, down_grad = jax.tree.map(
        lambda part: part.astype(jnp.float32),
        lax.psum_scatter(as_sent(rounded), "dp", scatter_dimension=0, tiled=True),
    )
    return (
        input_grad,
        gate_grad.astype(jnp.bfloat16),
        up_grad.astype(jnp.bfloat16),
        down_grad.astype(jnp.bfloat16),
    )


def solution(mesh):
    return jax.shard_map(
        body,
        mesh=mesh,
        in_specs=(
            P(("expert", "dp"), None),
            P(("expert", "dp"), None),
            P(("expert", "dp"), None),
            P(("expert", "dp"), None),
            P(("expert", "dp"), None),
            P("dp", "expert"),
            P("dp", "expert"),
            P("dp", "expert"),
        ),
        out_specs=(
            P(("expert", "dp"), None),
            P("dp", "expert"),
            P("dp", "expert"),
            P("dp", "expert"),
        ),
        check_vma=False,
    )
```

profile of v0, /device:TPU:0, one launch (start us, length us, event | category | flops | bytes accessed | tf_op | source)
XLA Modules:
  0.0 127.0 jit_solution(7504432330046653074)
XLA Ops:
  7.2 0.0 all-gather.8.cloned.1.call-start
  7.2 0.7 all-gather.8.cloned.1.call-update
  7.9 0.0 all-gather.6.cloned.1.call-start
  8.0 0.7 all-gather.6.cloned.1.call-update
  8.7 0.1 copy.29
  8.8 0.1 eq.95
  8.9 0.1 eq.85
  9.0 0.1 copy.30
  9.1 0.1 eq.99
  9.2 0.1 eq.91
  9.3 1.1 reduce-window.6
  10.5 0.2 slice_reduce_fusion
  10.7 0.2 reduce-window.9
  10.9 0.1 add_bitcast_fusion
  11.0 0.3 select_reduce_fusion
  11.3 0.1 copy.33
  11.4 0.1 reshape.217
  11.5 0.1 copy.40
  11.6 0.1 convert_element_type.88
  11.7 0.6 gather_fusion.2
  12.4 0.1 select_multiply_fusion
  12.5 0.1 broadcast_in_dim.21
  12.5 1.0 broadcast_in_dim.36
  13.5 8.3 %all-to-all-start.1 = ((bf16[16,5,3584]{2,1,0:T(8,128)(2,1)}), bf16[16,5,3584]{2,1,0:T(8,128)(2,1)S(1)}, u32[]{:S(2)}, u32[]{:S(2)}) async-start(bf16[16,5,3584]{2,1,0:T(8,128)(2,1)} %bitcast.3), calls=%async_computation.1 | async-start | bytes 1835008 | tf_op jit(solution)/shard_map/all_to_all | solution.py:93
  21.8 0.0 all-gather.4.cloned.1.call-start
  21.9 0.7 all-gather.4.cloned.1.call-update
  22.6 0.1 reshape.219
  22.7 0.6 gather_fusion.1
  23.3 0.1 copy.37
  23.4 0.1 convert_element_type.85
  23.5 0.1 copy.35
  23.6 0.1 reshape.218
  23.7 0.7 gather_fusion
  24.4 0.1 multiply_convert_fusion
  24.5 0.1 broadcast_in_dim.19
  24.6 19.3 %all-to-all-done.1 = bf16[16,5,3584]{2,1,0:T(8,128)(2,1)S(1)} async-done(((bf16[16,5,3584]{2,1,0:T(8,128)(2,1)}), bf16[16,5,3584]{2,1,0:T(8,128)(2,1)S(1)}, u32[]{:S(2)}, u32[]{:S(2)}) %all-to-all-start.1) | async-done | bytes 573472 | tf_op jit(solution)/shard_map/all_to_all | solution.py:93
  43.9 1.0 broadcast_in_dim.20
  44.9 5.4 %all-to-all-start = ((bf16[16,5,3584]{2,1,0:T(8,128)(2,1)}), bf16[16,5,3584]{2,1,0:T(8,128)(2,1)S(1)}, u32[]{:S(2)}, u32[]{:S(2)}) async-start(bf16[16,5,3584]{2,1,0:T(8,128)(2,1)} %bitcast.32), calls=%async_computation | async-start | bytes 1835008 | tf_op jit(solution)/shard_map/all_to_all | solution.py:94
  50.3 0.0 reduce-scatter.4.cloned.1.call-start
  50.3 0.2 all_to_all.27
  50.6 20.5 %all-to-all-done = bf16[16,5,3584]{2,1,0:T(8,128)(2,1)S(1)} async-done(((bf16[16,5,3584]{2,1,0:T(8,128)(2,1)}), bf16[16,5,3584]{2,1,0:T(8,128)(2,1)S(1)}, u32[]{:S(2)}, u32[]{:S(2)}) %all-to-all-start) | async-done | bytes 573472 | tf_op jit(solution)/shard_map/all_to_all | solution.py:94
  71.0 0.2 all_to_all.24
  71.3 0.0 all-gather.8.cloned.1.call-done
  71.3 2.3 %fusion.17 = f32[80,384]{1,0:T(8,128)S(1)} fusion(bf16[80,3584]{1,0:T(8,128)(2,1)S(1)} %all_to_all.27, bf16[3584,384]{1,0:T(8,128)(2,1)} %all-gather.8.cloned.1.call-done), kind=kOutput, calls=%fused_computation.52 | convolution fusion | flops 220200960 | bytes 3448832 | tf_op jit(solution)/shard_map/dot_general | solution.py:40
  73.7 0.0 all-gather.6.cloned.1.call-done
  73.7 2.3 %fusion.16 = f32[80,384]{1,0:T(8,128)S(1)} fusion(bf16[80,3584]{1,0:T(8,128)(2,1)S(1)} %all_to_all.27, bf16[3584,384]{1,0:T(8,128)(2,1)} %all-gather.6.cloned.1.call-done), kind=kOutput, calls=%fused_computation.51 | convolution fusion | flops 220200960 | bytes 3448832 | tf_op jit(solution)/shard_map/dot_general | solution.py:41
  76.0 0.0 all-gather.4.cloned.1.call-done
  76.1 2.4 %multiply_convert_fusion.2 = (bf16[80,384]{1,0:T(8,128)(2,1)S(1)}, bf16[80,384]{1,0:T(8,128)(2,1)S(1)}) fusion(f32[80,384]{1,0:T(8,128)S(1)} %fusion.17, f32[80,384]{1,0:T(8,128)S(1)} %fusion.16, bf16[80,3584]{1,0:T(8,128)(2,1)S(1)} %all_to_all.24, bf16[3584,384]{1,0:T(8,128)(2,1)} %all-gather.4.cloned.1.call-done), kind=kOutput, calls=%fused_computation.13 | convolution fusion | flops 220600320 | bytes 3694592 | tf_op jit(solution)/shard_map/dot_general | solution.py:44
  78.4 2.5 %convolution_convert_fusion.2 = bf16[3584,384]{1,0:T(8,128)(2,1)} fusion(bf16[80,3584]{1,0:T(8,128)(2,1)S(1)} %all_to_all.27, bf16[80,384]{1,0:T(8,128)(2,1)S(1)} %get-tuple-element.10), kind=kOutput, calls=%fused_computation.5 | convolution fusion | flops 221577216 | bytes 3387392 | tf_op jit(solution)/shard_map/dot_general | solution.py:56
  80.9 0.0 reduce-scatter.4.cloned.1.call-update
  80.9 0.0 reduce-scatter.6.cloned.1.call-start
  81.0 2.5 %convolution_convert_fusion.1 = bf16[3584,384]{1,0:T(8,128)(2,1)} fusion(bf16[80,3584]{1,0:T(8,128)(2,1)S(1)} %all_to_all.27, bf16[80,384]{1,0:T(8,128)(2,1)S(1)} %get-tuple-element.9), kind=kOutput, calls=%fused_computation.4 | convolution fusion | flops 221577216 | bytes 3387392 | tf_op jit(solution)/shard_map/dot_general | solution.py:57
  83.5 0.0 reduce-scatter.8.cloned.1.call-start
  83.6 2.6 %convolution_convert_fusion = bf16[3584,384]{1,0:T(8,128)(2,1)} fusion(bf16[80,3584]{1,0:T(8,128)(2,1)S(1)} %all_to_all.24, f32[80,384]{1,0:T(8,128)S(1)} %fusion.16, f32[80,384]{1,0:T(8,128)S(1)} %fusion.17), kind=kOutput, calls=%fused_computation.3 | convolution fusion | flops 221761536 | bytes 3571712 | tf_op jit(solution)/shard_map/dot_general | solution.py:58
  86.2 3.5 %fusion.18 = f32[80,3584]{1,0:T(8,128)S(1)} fusion(bf16[80,384]{1,0:T(8,128)(2,1)S(1)} %get-tuple-element.10, bf16[3584,384]{1,0:T(8,128)(2,1)} %all-gather.8.cloned.1.call-done), kind=kOutput, calls=%fused_computation.53 | convolution fusion | flops 220200960 | bytes 3960832 | tf_op jit(solution)/shard_map/dot_general | solution.py:48
  89.7 1.0 fusion
  90.7 1.2 all_to_all.28
  91.8 5.7 %all-to-all-start.2 = ((bf16[16,5,3584]{2,1,0:T(8,128)(2,1)}), bf16[16,5,3584]{2,1,0:T(8,128)(2,1)S(1)}, u32[]{:S(2)}, u32[]{:S(2)}) async-start(bf16[16,5,3584]{2,1,0:T(8,128)(2,1)} %all_to_all.28), calls=%async_computation.2 | async-start | bytes 1835008 | tf_op jit(solution)/shard_map/all_to_all | solution.py:97
  97.5 0.1 copy.34
  97.6 0.1 eq.103
  97.7 20.4 %all-to-all-done.2 = bf16[16,5,3584]{2,1,0:T(8,128)(2,1)S(1)} async-done(((bf16[16,5,3584]{2,1,0:T(8,128)(2,1)}), bf16[16,5,3584]{2,1,0:T(8,128)(2,1)S(1)}, u32[]{:S(2)}, u32[]{:S(2)}) %all-to-all-start.2) | async-done | bytes 573472 | tf_op jit(solution)/shard_map/all_to_all | solution.py:97
  118.0 0.2 convert_reduce_fusion
  118.2 0.1 reshape.220
  118.3 1.8 %convolution_convert_fusion.3 = bf16[128,3584]{1,0:T(8,128)(2,1)} fusion(f32[20,3584]{1,0:T(8,128)S(1)} %reshape.220, s32[20]{0:T(128)S(1)} %get-tuple-element.8, pred[20]{0:T(512)(128)(4,1)S(1)} %eq.103), kind=kOutput, calls=%fused_computation.6 | convolution fusion | flops 110564352 | bytes 1204324 | tf_op jit(solution)/shard_map/dot_general | solution.py:108
  (29 shorter events, 0.2 us)
Async XLA Ops:
  7.2 4.5 %copy-start = (bf16[128,3584]{1,0:T(8,128)(2,1)S(1)}, bf16[128,3584]{1,0:T(8,128)(2,1)}, u32[]{:S(2)}) copy-start(bf16[128,3584]{1,0:T(8,128)(2,1)} %param.10) | copy-start | bytes 2752516
  7.2 1.5 %copy-start.3 = (s32[128,8]{0,1:T(8,128)S(1)}, s32[128,8]{0,1:T(8,128)}, u32[]{:S(2)}) copy-start(s32[128,8]{0,1:T(8,128)} %param.12) | copy-start | bytes 12292
  7.2 1.8 %copy-start.5 = (s32[128,8]{0,1:T(8,128)S(1)}, s32[128,8]{0,1:T(8,128)}, u32[]{:S(2)}) copy-start(s32[128,8]{0,1:T(8,128)} %param.14) | copy-start | bytes 12292
  7.2 64.1 %all-gather.8.cloned.1.call-start = ((), (), s32[]{:S(2)}) async-start(), calls=%async_computation.8 | async-start | bytes 4128768 | tf_op jit(solution)/shard_map/all_gather | solution.py:71
  7.9 65.7 %all-gather.6.cloned.1.call-start = ((), (), s32[]{:S(2)}) async-start(), calls=%async_computation.7 | async-start | bytes 4128768 | tf_op jit(solution)/shard_map/all_gather | solution.py:72
  12.3 10.3 %copy-start.2 = (bf16[128,3584]{1,0:T(8,128)(2,1)S(1)}, bf16[128,3584]{1,0:T(8,128)(2,1)}, u32[]{:S(2)}) copy-start(bf16[128,3584]{1,0:T(8,128)(2,1)} %param.11) | copy-start | bytes 2752516
  12.5 11.0 %copy-start.4 = (f32[128,8]{0,1:T(8,128)S(1)}, f32[128,8]{0,1:T(8,128)}, u32[]{:S(2)}) copy-start(f32[128,8]{0,1:T(8,128)} %param.13) | copy-start | bytes 12292
  13.5 30.4 %all-to-all-start.1 = ((bf16[16,5,3584]{2,1,0:T(8,128)(2,1)}), bf16[16,5,3584]{2,1,0:T(8,128)(2,1)S(1)}, u32[]{:S(2)}, u32[]{:S(2)}) async-start(bf16[16,5,3584]{2,1,0:T(8,128)(2,1)} %bitcast.3), calls=%async_computation.1 | async-start | bytes 1835008 | tf_op jit(solution)/shard_map/all_to_all | solution.py:93
  21.8 54.2 %all-gather.4.cloned.1.call-start = ((), (), s32[]{:S(2)}) async-start(), calls=%async_computation.6 | async-start | bytes 4128768 | tf_op jit(solution)/shard_map/all_gather | solution.py:73
  44.9 26.2 %all-to-all-start = ((bf16[16,5,3584]{2,1,0:T(8,128)(2,1)}), bf16[16,5,3584]{2,1,0:T(8,128)(2,1)S(1)}, u32[]{:S(2)}, u32[]{:S(2)}) async-start(bf16[16,5,3584]{2,1,0:T(8,128)(2,1)} %bitcast.32), calls=%async_computation | async-start | bytes 1835008 | tf_op jit(solution)/shard_map/all_to_all | solution.py:94
  50.3 69.8 %reduce-scatter.4.cloned.1.call-start = ((), (), s32[]{:S(2)}) async-start(), calls=%async_computation.9 | async-start | bytes 4128768 | tf_op jit(solution)/shard_map/reduce_scatter | solution.py:119
  80.9 39.2 %reduce-scatter.6.cloned.1.call-start = ((), (), s32[]{:S(2)}) async-start(), calls=%async_computation.10 | async-start | bytes 4128768 | tf_op jit(solution)/shard_map/reduce_scatter | solution.py:119
  83.5 36.6 %reduce-scatter.8.cloned.1.call-start = ((), (), s32[]{:S(2)}) async-start(), calls=%async_computation.11 | async-start | bytes 4128768 | tf_op jit(solution)/shard_map/reduce_scatter | solution.py:119
  86.2 3.5 %copy-start.1 = (bf16[3584,384]{1,0:T(8,128)(2,1)S(1)}, bf16[3584,384]{1,0:T(8,128)(2,1)}, u32[]{:S(2)}) copy-start(bf16[3584,384]{1,0:T(8,128)(2,1)} %all-gather.6.cloned.1.call-done) | copy-start | bytes 8257540
  91.8 26.2 %all-to-all-start.2 = ((bf16[16,5,3584]{2,1,0:T(8,128)(2,1)}), bf16[16,5,3584]{2,1,0:T(8,128)(2,1)S(1)}, u32[]{:S(2)}, u32[]{:S(2)}) async-start(bf16[16,5,3584]{2,1,0:T(8,128)(2,1)} %all_to_all.28), calls=%async_computation.2 | async-start | bytes 1835008 | tf_op jit(solution)/shard_map/all_to_all | solution.py:97
Sparse Core Ops, SparseCore 0:
  9.6 14.2 all-gather.7
  25.4 12.7 all-gather.5
  39.7 12.7 all-gather.3
  81.0 10.2 reduce-scatter.3
  94.1 11.5 reduce-scatter.5
  108.3 11.5 reduce-scatter.7
where the time goes:
time: 127 us
  waiting for transfers between devices  62.3 us (49%)
  matrix products  20.9 us (16%)
  starting transfers between devices  19.6 us (15%)
  between operations  14.4 us (11%)
  local copies, waits for them, and re-layouts  7.64 us (6%)
  other arithmetic  2.14 us (2%)
    all_to_all x1, waiting for transfers between devices, body(): lax.all_to_all(copies_grad, 'expert', split_axis=0, concat_axis=0, tiled=...  20.5 us
    all_to_all x1, waiting for transfers between devices, body(): lax.all_to_all(partial_value, 'expert', split_axis=0, concat_axis=0, tile...  20.4 us
    all_to_all x1, waiting for transfers between devices, body(): lax.all_to_all(copies_in, 'expert', split_axis=0, concat_axis=0, tiled=True)  19.3 us
    all_to_all x1, starting transfers between devices, body(): lax.all_to_all(copies_in, 'expert', split_axis=0, concat_axis=0, tiled=True)  8.31 us
    all_to_all x1, starting transfers between devices, body(): lax.all_to_all(partial_value, 'expert', split_axis=0, concat_axis=0, tile...  5.65 us
    all_to_all x1, starting transfers between devices, body(): lax.all_to_all(copies_grad, 'expert', split_axis=0, concat_axis=0, tiled=...  5.42 us
    dot_general x1, matrix products, expert_backward(): lax.dot_general(gate_side, gate_full, across, preferred_element_type=jnp....  3.49 us
    dot_general x1, matrix products, expert_backward(): lax.dot_general(slot_grads, hidden, rows_first, preferred_element_type=jn...  2.57 us
  transfers between devices with their start and end apart: 9, of which 3 were waited for; matrix products, arithmetic and copies ran while one was open for 19% of the time, Pallas kernels for 0%

commit v1 on v0

v1 whole, which is shorter than its diff:
```python
import jax
import jax.numpy as jnp
from jax import lax
from jax.experimental import pallas as pl
from jax.experimental.pallas import tpu as pltpu
from jax.sharding import PartitionSpec as P

SPLIT = 4
MOST = 5
PIECE = 16
BACK = 8

F32 = jnp.float32
BF16 = jnp.bfloat16


def params(mib=40):
    return pltpu.CompilerParams(vmem_limit_bytes=mib * 1024 * 1024)


def cost(flops, moved):
    return pl.CostEstimate(flops=int(flops), bytes_accessed=int(moved), transcendentals=0)


def iota(shape, axis):
    return lax.broadcasted_iota(jnp.int32, shape, axis)


def dot(a, b, dims=((1,), (0,))):
    return lax.dot_general(a, b, (dims, ((), ())), preferred_element_type=F32)


def pick_rows(routes, keep, gates, expert, slot, valid):
    rows, tokens = expert.shape[0], routes.shape[1]
    chosen = jnp.zeros((rows, tokens), F32)
    gate = jnp.zeros((rows, tokens), F32)
    for k in range(routes.shape[0]):
        hit = (routes[k : k + 1, :] == expert) & (keep[k : k + 1, :] == 1)
        chosen = jnp.where(hit, 1.0, chosen)
        gate = jnp.where(hit, gates[k : k + 1, :], gate)
    upto = (iota((tokens, tokens), 0) <= iota((tokens, tokens), 1)).astype(BF16)
    rank = dot(chosen.astype(BF16), upto)
    hot = (chosen > 0.5) & (rank == (slot + 1).astype(F32)) & valid
    return hot, gate


def gather_kernel(live, where_ref, routes_ref, keep_ref, gates_ref, x_ref, o_ref, *outs):
    place = where_ref[0] // SPLIT
    me = where_ref[1]
    half = x_ref.shape[1] // 2
    pieces, back_ref = outs[:-1], outs[-1]
    routes, keep, gates = routes_ref[...], keep_ref[...], gates_ref[...]

    row = iota((live * PIECE, 1), 0)
    expert = lax.rem(place + row // PIECE, live)
    side = lax.rem(row, PIECE) // MOST
    slot = lax.rem(lax.rem(row, PIECE), MOST)
    hot, gate = pick_rows(routes, keep, gates, expert, slot, side < 2)
    hot_x = (hot & (side == 0)).astype(F32).astype(BF16)
    hot_s = hot & (side == 1)
    scale = jnp.sum(jnp.where(hot_s, gate, 0.0), axis=1, keepdims=True)
    hot_s = hot_s.astype(F32).astype(BF16)
    for q in range(2):
        start = pl.multiple_of((me ^ q) * half, 128)
        rows = dot(hot_x, x_ref[:, pl.ds(start, half)])
        rows = rows + scale * dot(hot_s, o_ref[:, pl.ds(start, half)])
        rows = rows.astype(BF16)
        for d in range(live):
            pieces[2 * d + q][...] = rows[d * PIECE : (d + 1) * PIECE]

    row = iota((live * BACK, 1), 0)
    expert = lax.rem(place + row // BACK, live)
    slot = lax.rem(row, BACK)
    hot, _ = pick_rows(routes, keep, gates, expert, slot, slot < MOST)
    back_ref[...] = hot.astype(F32)


def merge_kernel(live, where_ref, *refs):
    pieces, (x_ref, s_ref) = refs[:-2], refs[-2:]
    me = where_ref[1]
    rows = live * 2 * MOST
    stacked = jnp.concatenate([piece[...] for piece in pieces], axis=0)
    shape = (2 * rows, 2 * live * PIECE)
    out, source = iota(shape, 0), iota(shape, 1)
    side, at = out // rows, lax.rem(out, rows)
    d, replica, slot = at // (2 * MOST), lax.rem(at, 2 * MOST) // MOST, lax.rem(at, MOST)
    wanted = (2 * d + (replica ^ me)) * PIECE + side * MOST + slot
    merged = dot((source == wanted).astype(F32).astype(BF16), stacked).astype(BF16)
    x_ref[...] = merged[:rows]
    s_ref[...] = merged[rows:]


def partial_kernel(*refs):
    xs, ss = refs[:SPLIT], refs[SPLIT : 2 * SPLIT]
    gate_ref, up_ref, down_ref, out_ref = refs[2 * SPLIT :]
    x = jnp.concatenate([r[...] for r in xs], axis=0)
    s = jnp.concatenate([r[...] for r in ss], axis=0)
    width = gate_ref.shape[1]
    out = jnp.concatenate([dot(x, gate_ref[...]), dot(x, up_ref[...]), dot(s, down_ref[...])], axis=1)

    @pl.when(pl.program_id(0) == 0)
    def _():
        out_ref[...] = out

    @pl.when(pl.program_id(0) > 0)
    def _():
        out_ref[...] += out


def sides_kernel(mine_ref, other_ref, gate_ref, up_ref, *outs):
    parts, sides_ref = outs[:-1], outs[-1]
    width = gate_ref.shape[1]
    rows = mine_ref.shape[0] // SPLIT

    @pl.when(pl.program_id(0) == 0)
    def _():
        total = mine_ref[...] + other_ref[...]
        pre_gate, pre_up = total[:, :width], total[:, width : 2 * width]
        hidden_grad = total[:, 2 * width :]
        sigma = jax.nn.sigmoid(pre_gate)
        activated = pre_gate * sigma
        slope = sigma * (1.0 + pre_gate * (1.0 - sigma))
        sides_ref[:, :width] = (hidden_grad * pre_up * slope).astype(BF16)
        sides_ref[:, width : 2 * width] = (hidden_grad * activated).astype(BF16)
        sides_ref[:, 2 * width :] = (activated * pre_up).astype(BF16)

    across = ((1,), (1,))
    part = dot(sides_ref[:, :width], gate_ref[...], across)
    part = (part + dot(sides_ref[:, width : 2 * width], up_ref[...], across)).astype(BF16)
    for k in range(SPLIT):
        parts[k][...] = part[k * rows : (k + 1) * rows]


def grads_kernel(*refs):
    xs, ss = refs[:SPLIT], refs[SPLIT : 2 * SPLIT]
    sides_ref, gate_out, up_out, down_out = refs[2 * SPLIT :]
    width = gate_out.shape[1]
    x = jnp.concatenate([r[...] for r in xs], axis=0)
    s = jnp.concatenate([r[...] for r in ss], axis=0)
    first = ((0,), (0,))
    gate_out[...] = dot(x, sides_ref[:, :width], first).astype(BF16)
    up_out[...] = dot(x, sides_ref[:, width : 2 * width], first).astype(BF16)
    down_out[...] = dot(s, sides_ref[:, 2 * width :], first).astype(BF16)


def sum_kernel(live, where_ref, *refs):
    parts, outs = refs[:SPLIT], refs[SPLIT:]
    me = where_ref[1]
    total = parts[0][...].astype(F32)
    for part in parts[1:]:
        total = total + part[...].astype(F32)
    total = total.astype(BF16)
    rows = live * 2 * MOST
    shape = (2 * live * BACK, rows)
    out, source = iota(shape, 0), iota(shape, 1)
    d, q, slot = out // (2 * BACK), lax.rem(out, 2 * BACK) // BACK, lax.rem(out, BACK)
    wanted = d * 2 * MOST + (q ^ me) * MOST + slot
    take = (source == wanted) & (slot < MOST)
    moved = dot(take.astype(F32).astype(BF16), total)
    for piece in range(2 * live):
        outs[piece][...] = moved[piece * BACK : (piece + 1) * BACK].astype(BF16)


def place_kernel(live, where_ref, hot_ref, *refs):
    pieces, out_ref = refs[:-1], refs[-1]
    me = where_ref[1]
    half = out_ref.shape[1] // 2
    hot = hot_ref[...].astype(BF16)
    for q in range(2):
        rows = jnp.concatenate([pieces[2 * d + q][...].astype(F32) for d in range(live)], axis=0)
        start = pl.multiple_of((me ^ q) * half, 128)
        out_ref[:, pl.ds(start, half)] = dot(hot, rows.astype(BF16), ((0,), (0,))).astype(BF16)


def like(shape, dtype):
    return jax.ShapeDtypeStruct(shape, dtype)


def body(
    layer_input, out_grad, routes, gate_values, keep_mask, gate_weight, up_weight, down_transposed
):
    devices, cores = lax.axis_size("expert"), lax.axis_size("dp")
    live = devices // SPLIT
    tokens, model = layer_input.shape
    half, width = gate_weight.shape
    where = jnp.stack([lax.axis_index("expert"), lax.axis_index("dp")]).astype(jnp.int32)
    smem, vmem = pl.BlockSpec(memory_space=pltpu.SMEM), pl.BlockSpec(memory_space=pltpu.VMEM)
    rows = 2 * live * MOST
    total = SPLIT * rows

    def to_source(d, q, forth):
        moved = []
        for i in range(devices):
            for r in range(cores):
                g, m = (i // SPLIT + d) % live, i % SPLIT
                there = (g * SPLIT + m) * cores + (r ^ q)
                here = i * cores + r
                moved.append((here, there) if forth else (there, here))
        return moved

    def in_plane(k):
        return [(i, (i // SPLIT) * SPLIT + ((i % SPLIT) ^ k)) for i in range(devices)]

    def travel(pieces, forth):
        out = []
        for d in range(live):
            for q in range(2):
                piece = pieces[2 * d + q]
                if d or q:
                    piece = lax.ppermute(piece, ("expert", "dp"), to_source(d, q, forth))
                out.append(piece)
        return out

    gathered = pl.pallas_call(
        lambda *refs: gather_kernel(live, *refs),
        out_shape=[like((PIECE, half), BF16)] * (2 * live) + [like((live * BACK, tokens), F32)],
        in_specs=[smem] + [vmem] * 5,
        out_specs=[vmem] * (2 * live + 1),
        compiler_params=params(),
        name="gather_rows",
    )(where, routes.T, keep_mask.T, gate_values.T, layer_input, out_grad)
    pieces, hot = gathered[:-1], gathered[-1]
    pieces = travel(pieces, True)
    x_own, s_own = pl.pallas_call(
        lambda *refs: merge_kernel(live, *refs),
        out_shape=[like((rows, half), BF16)] * 2,
        in_specs=[smem] + [vmem] * (2 * live),
        out_specs=[vmem] * 2,
        compiler_params=params(),
        name="merge_rows",
    )(where, *pieces)
    xs = [x_own] + [lax.ppermute(x_own, "expert", in_plane(k)) for k in range(1, SPLIT)]
    ss = [s_own] + [lax.ppermute(s_own, "expert", in_plane(k)) for k in range(1, SPLIT)]

    chunk = 256
    steps = half // chunk
    row_block = pl.BlockSpec((rows, chunk), lambda j: (0, j))
    weight_block = pl.BlockSpec((chunk, width), lambda j: (j, 0))
    whole = pl.BlockSpec((total, 3 * width), lambda j: (0, 0))
    mine = pl.pallas_call(
        partial_kernel,
        out_shape=like((total, 3 * width), F32),
        grid=(steps,),
        in_specs=[row_block] * (2 * SPLIT) + [weight_block] * 3,
        out_specs=whole,
        compiler_params=params(),
        cost_estimate=cost(6 * total * half * width, 6 * half * width + 4 * total * half),
        name="partial_products",
    )(*xs, *ss, gate_weight, up_weight, down_transposed)
    other = lax.ppermute(mine, "dp", [(r, r ^ 1) for r in range(cores)])
    sided = pl.pallas_call(
        sides_kernel,
        out_shape=[like((rows, half), BF16)] * SPLIT + [like((total, 3 * width), BF16)],
        grid=(steps,),
        in_specs=[whole] * 2 + [weight_block] * 2,
        out_specs=[row_block] * SPLIT + [whole],
        compiler_params=params(),
        cost_estimate=cost(4 * total * half * width, 4 * half * width + 2 * total * half),
        name="sides_and_parts",
    )(mine, other, gate_weight, up_weight)
    parts, sides = sided[:-1], sided[-1]
    parts = [parts[0]] + [lax.ppermute(parts[k], "expert", in_plane(k)) for k in range(1, SPLIT)]
    gate_grad, up_grad, down_grad = pl.pallas_call(
        grads_kernel,
        out_shape=[like((half, width), BF16)] * 3,
        grid=(steps,),
        in_specs=[row_block] * (2 * SPLIT) + [whole],
        out_specs=[weight_block] * 3,
        compiler_params=params(),
        cost_estimate=cost(6 * total * half * width, 6 * half * width + 4 * total * half),
        name="weight_grads",
    )(*xs, *ss, sides)
    returned = pl.pallas_call(
        lambda *refs: sum_kernel(live, *refs),
        out_shape=[like((BACK, half), BF16)] * (2 * live),
        in_specs=[smem] + [vmem] * SPLIT,
        out_specs=[vmem] * (2 * live),
        compiler_params=params(),
        name="sum_parts",
    )(where, *parts)
    returned = travel(returned, False)
    input_grad = pl.pallas_call(
        lambda *refs: place_kernel(live, *refs),
        out_shape=like((tokens, model), BF16),
        in_specs=[smem] + [vmem] * (2 * live + 1),
        out_specs=vmem,
        compiler_params=params(),
        name="place_rows",
    )(where, hot, *returned)
    return (input_grad, gate_grad, up_grad, down_grad)


def solution(mesh):
    return jax.shard_map(
        body,
        mesh=mesh,
        in_specs=(
            P(("expert", "dp"), None),
            P(("expert", "dp"), None),
            P(("expert", "dp"), None),
            P(("expert", "dp"), None),
            P(("expert", "dp"), None),
            P("dp", "expert"),
            P("dp", "expert"),
            P("dp", "expert"),
        ),
        out_specs=(
            P(("expert", "dp"), None),
            P("dp", "expert"),
            P("dp", "expert"),
            P("dp", "expert"),
        ),
        check_vma=False,
    )
```

time: 127 us -> 73.9 us (0.58)
  waiting for transfers between devices: 62.3 us -> 21.7 us
  matrix products: 20.9 us -> 0 us
  Pallas kernels: 0 us -> 14.2 us
  between operations: 14.4 us -> 0.74 us
  starting transfers between devices: 19.6 us -> 29.7 us
  other arithmetic: 2.14 us -> 0.08 us
    all_to_all x3 -> x0, waiting for transfers between devices: 60.1 us -> none  [the longest x1 20.5 us: body(): lax.all_to_all(copies_grad, 'expert', split_axis=0, concat_axis=0, tiled=...]
    ppermute x0 -> x24, starting transfers between devices: none -> 29.7 us  [the longest x14 17 us: travel(): piece = lax.ppermute(piece, ('expert', 'dp'), to_source(d, q, forth))]
    ppermute x0 -> x24, waiting for transfers between devices: none -> 21.7 us  [the longest x3 6.37 us: body(): lax.ppermute(parts[k], 'expert', in_plane(k))]
    dot_general x9 -> x0, matrix products: 20.9 us -> none  [the longest x1 3.49 us: expert_backward(): lax.dot_general(gate_side, gate_full, across, preferred_element_type=jnp....]
    all_to_all x3 -> x0, starting transfers between devices: 19.4 us -> none  [the longest x1 8.31 us: body(): lax.all_to_all(copies_in, 'expert', split_axis=0, concat_axis=0, tiled=True)]
    pallas_call x0 -> x7, Pallas kernels: none -> 14.2 us  [the longest x1 4.66 us: body(): pl.pallas_call(grads_kernel, out_shape=[like((half, width), BF16)] * 3, g...]
    unnamed x16, local copies, waits for them, and re-layouts: 0.35 us -> 7.19 us
    unnamed x6 -> x0, waiting for transfers between devices: 2.11 us -> none
  transfers between devices with their start and end apart: 9 -> 24, of which waited for: 3 -> 11; matrix products, arithmetic and copies ran while one was open for 19% -> 0% of each run, Pallas kernels for 0% -> 6%
where the time goes in v1:
time: 73.9 us; the launch traced here: 73.6 us
  starting transfers between devices  29.7 us (40%)
  waiting for transfers between devices  21.7 us (29%)
  Pallas kernels  14.2 us (19%)
  local copies, waits for them, and re-layouts  7.19 us (10%)
  between operations  0.74 us (1%)
    ppermute x14, starting transfers between devices, travel(): piece = lax.ppermute(piece, ('expert', 'dp'), to_source(d, q, forth))  17 us
    unnamed x16, local copies, waits for them, and re-layouts  7.19 us
    ppermute x3, waiting for transfers between devices, body(): lax.ppermute(parts[k], 'expert', in_plane(k))  6.37 us
    ppermute x14, waiting for transfers between devices, travel(): piece = lax.ppermute(piece, ('expert', 'dp'), to_source(d, q, forth))  5.94 us
    ppermute x3, starting transfers between devices, body(): lax.ppermute(x_own, 'expert', in_plane(k))  5.56 us
    ppermute x3, waiting for transfers between devices, body(): lax.ppermute(x_own, 'expert', in_plane(k))  5.56 us
    pallas_call x1, Pallas kernels, body(): pl.pallas_call(grads_kernel, out_shape=[like((half, width), BF16)] * 3, g...  4.66 us
    ppermute x3, starting transfers between devices, body(): lax.ppermute(s_own, 'expert', in_plane(k))  3.55 us
  transfers between devices with their start and end apart: 24, of which 11 were waited for; matrix products, arithmetic and copies ran while one was open for 0% of the time, Pallas kernels for 6%

profile of v1, /device:TPU:0, one launch (start us, length us, event | category | flops | bytes accessed | tf_op | source)
XLA Modules:
  0.0 73.6 jit_solution(14755231315544007792)
XLA Ops:
  0.6 0.0 copy-start
  0.6 0.1 pad_add_fusion.refs_0_
  0.7 1.3 %copy-done.3 = bf16[128,3584]{1,0:T(8,128)(2,1)S(1)} copy-done((bf16[128,3584]{1,0:T(8,128)(2,1)S(1)}, bf16[128,3584]{1,0:T(8,128)(2,1)}, u32[]{:S(2)}) %copy-start.3) | copy-done | bytes 917528
  2.0 1.2 %copy-done.4 = bf16[128,3584]{1,0:T(8,128)(2,1)S(1)} copy-done((bf16[128,3584]{1,0:T(8,128)(2,1)S(1)}, bf16[128,3584]{1,0:T(8,128)(2,1)}, u32[]{:S(2)}) %copy-start.4) | copy-done | bytes 917528
  3.2 0.7 copy-done.5
  3.9 0.7 copy-done.6
  4.5 0.7 copy-done.7
  5.2 1.1 %gather_rows.1 = (bf16[16,1792]{1,0:T(8,128)(2,1)S(1)}, bf16[16,1792]{1,0:T(8,128)(2,1)S(1)}, bf16[16,1792]{1,0:T(8,128)(2,1)S(1)}, bf16[16,1792]{1,0:T(8,128)(2...) custom-call(s32[2]{0:T(128)S(1)} %pad_add_fusion.refs_0_, ...), custom_call_target="tpu_custom_call" | custom-call | tf_op jit(solution)/shard_map/gather_rows/pallas_call | solution.py:214
  6.4 0.5 collective-permute-start
  6.9 2.6 %collective-permute-start.1 = (bf16[16,1792]{1,0:T(8,128)(2,1)S(1)}, bf16[16,1792]{1,0:T(8,128)(2,1)S(1)}, u32[]{:S(2)}, u32[]{:S(2)}) collective-permute-start(bf16[16,1792]{1,0:T(8,128)(2,1)S(1)} %get-tuple-element.34), channel_id=1, source_target_pairs={{0,8},{1,9},{2,10},{3,11},{4,12},{5,13},{6,14},{7,15},{8,16},{9,17... | collective-permute-start | bytes 172040 | tf_op jit(solution)/shard_map/ppermute | solution.py:210
  9.5 1.3 %collective-permute-start.2 = (bf16[16,1792]{1,0:T(8,128)(2,1)S(1)}, bf16[16,1792]{1,0:T(8,128)(2,1)S(1)}, u32[]{:S(2)}, u32[]{:S(2)}) collective-permute-start(bf16[16,1792]{1,0:T(8,128)(2,1)S(1)} %get-tuple-element.35), channel_id=1, source_target_pairs={{0,9},{1,8},{2,11},{3,10},{4,13},{5,12},{6,15},{7,14},{8,17},{9,16... | collective-permute-start | bytes 172040 | tf_op jit(solution)/shard_map/ppermute | solution.py:210
  10.9 1.3 %collective-permute-start.3 = (bf16[16,1792]{1,0:T(8,128)(2,1)S(1)}, bf16[16,1792]{1,0:T(8,128)(2,1)S(1)}, u32[]{:S(2)}, u32[]{:S(2)}) collective-permute-start(bf16[16,1792]{1,0:T(8,128)(2,1)S(1)} %get-tuple-element.36), channel_id=1, source_target_pairs={{0,16},{1,17},{2,18},{3,19},{4,20},{5,21},{6,22},{7,23},{8,24},{9,... | collective-permute-start | bytes 172040 | tf_op jit(solution)/shard_map/ppermute | solution.py:210
  12.2 1.3 %collective-permute-start.4 = (bf16[16,1792]{1,0:T(8,128)(2,1)S(1)}, bf16[16,1792]{1,0:T(8,128)(2,1)S(1)}, u32[]{:S(2)}, u32[]{:S(2)}) collective-permute-start(bf16[16,1792]{1,0:T(8,128)(2,1)S(1)} %get-tuple-element.37), channel_id=1, source_target_pairs={{0,17},{1,16},{2,19},{3,18},{4,21},{5,20},{6,23},{7,22},{8,25},{9,... | collective-permute-start | bytes 172040 | tf_op jit(solution)/shard_map/ppermute | solution.py:210
  13.4 0.0 collective-permute-done.refs_2_
  13.5 2.2 %collective-permute-start.5 = (bf16[16,1792]{1,0:T(8,128)(2,1)S(1)}, bf16[16,1792]{1,0:T(8,128)(2,1)S(1)}, u32[]{:S(2)}, u32[]{:S(2)}) collective-permute-start(bf16[16,1792]{1,0:T(8,128)(2,1)S(1)} %get-tuple-element.38), channel_id=1, source_target_pairs={{0,24},{1,25},{2,26},{3,27},{4,28},{5,29},{6,30},{7,31},{8,0},{9,1... | collective-permute-start | bytes 172040 | tf_op jit(solution)/shard_map/ppermute | solution.py:210
  15.7 0.0 collective-permute-done.1.refs_3_
  15.7 0.3 collective-permute-start.6
  16.0 0.0 collective-permute-done.2.refs_4_
  16.0 3.3 %collective-permute-done.3.refs_5_ = bf16[16,1792]{1,0:T(8,128)(2,1)S(1)} collective-permute-done((bf16[16,1792]{1,0:T(8,128)(2,1)S(1)}, bf16[16,1792]{1,0:T(8,128)(2,1)S(1)}, u32[]{:S(2)}, u32[]{:S(2)}) %collective-permute-start.3) | collective-permute-done | bytes 57376 | tf_op jit(solution)/shard_map/ppermute | solution.py:210
  19.3 1.2 %collective-permute-done.4.refs_6_ = bf16[16,1792]{1,0:T(8,128)(2,1)S(1)} collective-permute-done((bf16[16,1792]{1,0:T(8,128)(2,1)S(1)}, bf16[16,1792]{1,0:T(8,128)(2,1)S(1)}, u32[]{:S(2)}, u32[]{:S(2)}) %collective-permute-start.4) | collective-permute-done | bytes 57376 | tf_op jit(solution)/shard_map/ppermute | solution.py:210
  20.5 0.0 collective-permute-done.5.refs_7_
  20.5 1.2 %collective-permute-done.6.refs_8_ = bf16[16,1792]{1,0:T(8,128)(2,1)S(1)} collective-permute-done((bf16[16,1792]{1,0:T(8,128)(2,1)S(1)}, bf16[16,1792]{1,0:T(8,128)(2,1)S(1)}, u32[]{:S(2)}, u32[]{:S(2)}) %collective-permute-start.6) | collective-permute-done | bytes 57376 | tf_op jit(solution)/shard_map/ppermute | solution.py:210
  21.6 0.8 %merge_rows.1 = (bf16[40,1792]{1,0:T(8,128)(2,1)S(1)}, bf16[40,1792]{1,0:T(8,128)(2,1)S(1)}) custom-call(s32[2]{0:T(128)S(1)} %pad_add_fusion.refs_0_, bf16[16,1792]{1,0:T(8,128)(2,1)S(1)} %get-tuple-element.32.refs_1_, bf16[16,1792]{1,0:T(8,128)(2,1)S(1)} %collective-permute-done.refs_2_, bf16[16,1792]{1,0:T(8,128)(2,1)S(1)} %collective-permute-done.1.refs_3_, ...), custom_call_target="tpu_custom_call" | custom-call | tf_op jit(solution)/shard_map/merge_rows/pallas_call | solution.py:224
  22.5 1.6 %collective-permute-start.10 = (bf16[40,1792]{1,0:T(8,128)(2,1)S(1)}, bf16[40,1792]{1,0:T(8,128)(2,1)S(1)}, u32[]{:S(2)}, u32[]{:S(2)}) collective-permute-start(bf16[40,1792]{1,0:T(8,128)(2,1)S(1)} %get-tuple-element.41.refs_4_), channel_id=1, source_target_pairs={{0,2},{2,0},{4,6},{6,4},{8,10},{10,8},{12,14},{14,12},{16,18},{18,... | collective-permute-start | bytes 430088 | tf_op jit(solution)/shard_map/ppermute | solution.py:233
  24.0 1.5 %collective-permute-start.11 = (bf16[40,1792]{1,0:T(8,128)(2,1)S(1)}, bf16[40,1792]{1,0:T(8,128)(2,1)S(1)}, u32[]{:S(2)}, u32[]{:S(2)}) collective-permute-start(bf16[40,1792]{1,0:T(8,128)(2,1)S(1)} %get-tuple-element.41.refs_4_), channel_id=1, source_target_pairs={{0,4},{2,6},{4,0},{6,2},{8,12},{10,14},{12,8},{14,10},{16,20},{18,... | collective-permute-start | bytes 430088 | tf_op jit(solution)/shard_map/ppermute | solution.py:233
  25.5 0.5 collective-permute-start.12
  26.0 1.5 %collective-permute-start.7 = (bf16[40,1792]{1,0:T(8,128)(2,1)S(1)}, bf16[40,1792]{1,0:T(8,128)(2,1)S(1)}, u32[]{:S(2)}, u32[]{:S(2)}) collective-permute-start(bf16[40,1792]{1,0:T(8,128)(2,1)S(1)} %get-tuple-element.40.refs_0_), channel_id=1, source_target_pairs={{0,2},{2,0},{4,6},{6,4},{8,10},{10,8},{12,14},{14,12},{16,18},{18,... | collective-permute-start | bytes 430088 | tf_op jit(solution)/shard_map/ppermute | solution.py:232
  27.5 1.5 %collective-permute-start.8 = (bf16[40,1792]{1,0:T(8,128)(2,1)S(1)}, bf16[40,1792]{1,0:T(8,128)(2,1)S(1)}, u32[]{:S(2)}, u32[]{:S(2)}) collective-permute-start(bf16[40,1792]{1,0:T(8,128)(2,1)S(1)} %get-tuple-element.40.refs_0_), channel_id=1, source_target_pairs={{0,4},{2,6},{4,0},{6,2},{8,12},{10,14},{12,8},{14,10},{16,20},{18,... | collective-permute-start | bytes 430088 | tf_op jit(solution)/shard_map/ppermute | solution.py:232
  29.0 0.0 collective-permute-done.10.refs_5_
  29.0 2.6 %collective-permute-start.9 = (bf16[40,1792]{1,0:T(8,128)(2,1)S(1)}, bf16[40,1792]{1,0:T(8,128)(2,1)S(1)}, u32[]{:S(2)}, u32[]{:S(2)}) collective-permute-start(bf16[40,1792]{1,0:T(8,128)(2,1)S(1)} %get-tuple-element.40.refs_0_), channel_id=1, source_target_pairs={{0,6},{2,4},{4,2},{6,0},{8,14},{10,12},{12,10},{14,8},{16,22},{18,... | collective-permute-start | bytes 430088 | tf_op jit(solution)/shard_map/ppermute | solution.py:232
  31.6 1.6 %collective-permute-done.11.refs_6_ = bf16[40,1792]{1,0:T(8,128)(2,1)S(1)} collective-permute-done((bf16[40,1792]{1,0:T(8,128)(2,1)S(1)}, bf16[40,1792]{1,0:T(8,128)(2,1)S(1)}, u32[]{:S(2)}, u32[]{:S(2)}) %collective-permute-start.11) | collective-permute-done | bytes 143392 | tf_op jit(solution)/shard_map/ppermute | solution.py:233
  33.2 0.0 collective-permute-done.12.refs_7_
  33.2 2.1 %collective-permute-done.7.refs_1_ = bf16[40,1792]{1,0:T(8,128)(2,1)S(1)} collective-permute-done((bf16[40,1792]{1,0:T(8,128)(2,1)S(1)}, bf16[40,1792]{1,0:T(8,128)(2,1)S(1)}, u32[]{:S(2)}, u32[]{:S(2)}) %collective-permute-start.7) | collective-permute-done | bytes 143392 | tf_op jit(solution)/shard_map/ppermute | solution.py:232
  35.3 3.4 %collective-permute-done.8.refs_2_ = bf16[40,1792]{1,0:T(8,128)(2,1)S(1)} collective-permute-done((bf16[40,1792]{1,0:T(8,128)(2,1)S(1)}, bf16[40,1792]{1,0:T(8,128)(2,1)S(1)}, u32[]{:S(2)}, u32[]{:S(2)}) %collective-permute-start.8) | collective-permute-done | bytes 143392 | tf_op jit(solution)/shard_map/ppermute | solution.py:232
  38.7 0.0 collective-permute-done.9.refs_3_
  38.7 1.3 %copy-done.1 = bf16[1792,384]{1,0:T(8,128)(2,1)S(1)} copy-done((bf16[1792,384]{1,0:T(8,128)(2,1)S(1)}, bf16[1792,384]{1,0:T(8,128)(2,1)}, u32[]{:S(2)}) %copy-start.1) | copy-done | bytes 1376280
  40.1 1.3 %copy-done.2 = bf16[1792,384]{1,0:T(8,128)(2,1)S(1)} copy-done((bf16[1792,384]{1,0:T(8,128)(2,1)S(1)}, bf16[1792,384]{1,0:T(8,128)(2,1)}, u32[]{:S(2)}) %copy-start.2) | copy-done | bytes 1376280
  41.4 2.7 %partial_products.1.mine_ref = f32[160,1152]{1,0:T(8,128)S(1)} custom-call(bf16[40,1792]{1,0:T(8,128)(2,1)S(1)} %get-tuple-element.40.refs_0_, bf16[40,1792]{1,0:T(8,128)(2,1)S(1)} %collective-permute-done.7.refs_1_, bf16[40,1792]{1,0:T(8,128)(2,1)S(1)} %collective-permute-done.8.refs_2_, bf16[40,1792]{1,0:T(8,128)(2,1)S(1)} %collective-permute-done.9.refs_3_, ...), custom_call_target="tpu_custom_call" | custom-call | flops 660602880 | bytes 5275648 | tf_op jit(solution)/shard_map/partial_products/pallas_call | solution.py:240
  44.2 0.1 collective-permute-start.13
  44.2 2.2 %collective-permute-done.13.other_ref = f32[160,1152]{1,0:T(8,128)S(1)} collective-permute-done((f32[160,1152]{1,0:T(8,128)S(1)}, f32[160,1152]{1,0:T(8,128)S(1)}, u32[]{:S(2)}, u32[]{:S(2)}) %collective-permute-start.13) | collective-permute-done | bytes 737312 | tf_op jit(solution)/shard_map/ppermute | solution.py:250
  46.4 2.2 %sides_and_parts.1 = (bf16[40,1792]{1,0:T(8,128)(2,1)S(1)}, bf16[40,1792]{1,0:T(8,128)(2,1)S(1)}, bf16[40,1792]{1,0:T(8,128)(2,1)S(1)}, bf16[40,1792]{1,0:T(8,128)(2,1)S(1)}, bf16[160,1152]{1,0:T(8,128)(2,1)S(1)}) custom-call(f32[160,1152]{1,0:T(8,128)S(1)} %partial_products.1.mine_ref, f32[160,1152]{1,0:T(8,128)S(1)} %collective-permute-done.13.other_ref, ...), custom_call_target="tpu_custom_call" | custom-call | flops 440401920 | bytes 3325952 | tf_op jit(solution)/shard_map/sides_and_parts/pallas_call | solution.py:251
  48.7 1.3 %collective-permute-start.14 = (bf16[40,1792]{1,0:T(8,128)(2,1)S(1)}, bf16[40,1792]{1,0:T(8,128)(2,1)S(1)}, u32[]{:S(2)}, u32[]{:S(2)}) collective-permute-start(bf16[40,1792]{1,0:T(8,128)(2,1)S(1)} %get-tuple-element.43), channel_id=1, source_target_pairs={{0,2},{2,0},{4,6},{6,4},{8,10},{10,8},{12,14},{14,12},{16,18},{18,... | collective-permute-start | bytes 430088 | tf_op jit(solution)/shard_map/ppermute | solution.py:262
  50.0 0.8 %collective-permute-start.15 = (bf16[40,1792]{1,0:T(8,128)(2,1)S(1)}, bf16[40,1792]{1,0:T(8,128)(2,1)S(1)}, u32[]{:S(2)}, u32[]{:S(2)}) collective-permute-start(bf16[40,1792]{1,0:T(8,128)(2,1)S(1)} %get-tuple-element.44), channel_id=1, source_target_pairs={{0,4},{2,6},{4,0},{6,2},{8,12},{10,14},{12,8},{14,10},{16,20},{18,... | collective-permute-start | bytes 430088 | tf_op jit(solution)/shard_map/ppermute | solution.py:262
  50.8 1.4 %collective-permute-start.16 = (bf16[40,1792]{1,0:T(8,128)(2,1)S(1)}, bf16[40,1792]{1,0:T(8,128)(2,1)S(1)}, u32[]{:S(2)}, u32[]{:S(2)}) collective-permute-start(bf16[40,1792]{1,0:T(8,128)(2,1)S(1)} %get-tuple-element.45), channel_id=1, source_target_pairs={{0,6},{2,4},{4,2},{6,0},{8,14},{10,12},{12,10},{14,8},{16,22},{18,... | collective-permute-start | bytes 430088 | tf_op jit(solution)/shard_map/ppermute | solution.py:262
  52.2 3.1 %collective-permute-done.14.refs_2_ = bf16[40,1792]{1,0:T(8,128)(2,1)S(1)} collective-permute-done((bf16[40,1792]{1,0:T(8,128)(2,1)S(1)}, bf16[40,1792]{1,0:T(8,128)(2,1)S(1)}, u32[]{:S(2)}, u32[]{:S(2)}) %collective-permute-start.14) | collective-permute-done | bytes 143392 | tf_op jit(solution)/shard_map/ppermute | solution.py:262
  55.3 1.6 %collective-permute-done.15.refs_3_ = bf16[40,1792]{1,0:T(8,128)(2,1)S(1)} collective-permute-done((bf16[40,1792]{1,0:T(8,128)(2,1)S(1)}, bf16[40,1792]{1,0:T(8,128)(2,1)S(1)}, u32[]{:S(2)}, u32[]{:S(2)}) %collective-permute-start.15) | collective-permute-done | bytes 143392 | tf_op jit(solution)/shard_map/ppermute | solution.py:262
  56.9 1.6 %collective-permute-done.16.refs_4_ = bf16[40,1792]{1,0:T(8,128)(2,1)S(1)} collective-permute-done((bf16[40,1792]{1,0:T(8,128)(2,1)S(1)}, bf16[40,1792]{1,0:T(8,128)(2,1)S(1)}, u32[]{:S(2)}, u32[]{:S(2)}) %collective-permute-start.16) | collective-permute-done | bytes 143392 | tf_op jit(solution)/shard_map/ppermute | solution.py:262
  58.6 0.8 %sum_parts.1 = (bf16[8,1792]{1,0:T(8,128)(2,1)S(1)}, bf16[8,1792]{1,0:T(8,128)(2,1)S(1)}, bf16[8,1792]{1,0:T(8,128)(2,1)S(1)}, bf16[8,1792]{1,0:T(8,128)(2,1)S(1...) custom-call(s32[2]{0:T(128)S(1)} %pad_add_fusion.refs_0_, ...), custom_call_target="tpu_custom_call" | custom-call | tf_op jit(solution)/shard_map/sum_parts/pallas_call | solution.py:273
  59.4 0.1 collective-permute-start.17
  59.5 2.7 %collective-permute-start.18 = (bf16[8,1792]{1,0:T(8,128)(2,1)S(1)}, bf16[8,1792]{1,0:T(8,128)(2,1)S(1)}, u32[]{:S(2)}, u32[]{:S(2)}) collective-permute-start(bf16[8,1792]{1,0:T(8,128)(2,1)S(1)} %get-tuple-element.48), channel_id=1, source_target_pairs={{8,0},{9,1},{10,2},{11,3},{12,4},{13,5},{14,6},{15,7},{16,8},{17,9... | collective-permute-start | bytes 86024 | tf_op jit(solution)/shard_map/ppermute | solution.py:210
  62.2 0.1 collective-permute-start.19
  62.3 0.6 collective-permute-start.20
  62.8 1.8 %collective-permute-start.21 = (bf16[8,1792]{1,0:T(8,128)(2,1)S(1)}, bf16[8,1792]{1,0:T(8,128)(2,1)S(1)}, u32[]{:S(2)}, u32[]{:S(2)}) collective-permute-start(bf16[8,1792]{1,0:T(8,128)(2,1)S(1)} %get-tuple-element.51), channel_id=1, source_target_pairs={{17,0},{16,1},{19,2},{18,3},{21,4},{20,5},{23,6},{22,7},{25,8},{24... | collective-permute-start | bytes 86024 | tf_op jit(solution)/shard_map/ppermute | solution.py:210
  64.7 0.0 collective-permute-done.17.refs_3_
  64.7 1.9 %collective-permute-start.22 = (bf16[8,1792]{1,0:T(8,128)(2,1)S(1)}, bf16[8,1792]{1,0:T(8,128)(2,1)S(1)}, u32[]{:S(2)}, u32[]{:S(2)}) collective-permute-start(bf16[8,1792]{1,0:T(8,128)(2,1)S(1)} %get-tuple-element.52), channel_id=1, source_target_pairs={{24,0},{25,1},{26,2},{27,3},{28,4},{29,5},{30,6},{31,7},{0,8},{1,9... | collective-permute-start | bytes 86024 | tf_op jit(solution)/shard_map/ppermute | solution.py:210
  66.6 0.0 collective-permute-done.18.refs_4_
  66.6 0.1 collective-permute-start.23
  66.7 4.7 %weight_grads.1 = (bf16[1792,384]{1,0:T(8,128)(2,1)}, bf16[1792,384]{1,0:T(8,128)(2,1)}, bf16[1792,384]{1,0:T(8,128)(2,1)}) custom-call(bf16[40,1792]{1,0:T(8,128)(2,1)S(1)} %get-tuple-element.40.refs_0_, bf16[40,1792]{1,0:T(8,128)(2,1)S(1)} %collective-permute-done.7.refs_1_, bf16[40,1792]{1,0:T(8,128)(2,1)S(1)} %collective-permute-done.8.refs_2_, ...), custom_call_target="tpu_custom_call" | custom-call | flops 660602880 | bytes 5275648 | tf_op jit(solution)/shard_map/weight_grads/pallas_call | solution.py:263
  71.4 0.0 collective-permute-done.19.refs_5_
  71.4 0.0 collective-permute-done.20.refs_6_
  71.4 0.0 collective-permute-done.21.refs_7_
  71.4 0.0 collective-permute-done.22.refs_8_
  71.4 0.3 collective-permute-done.23.refs_9_
  71.7 1.9 %place_rows.1 = bf16[128,3584]{1,0:T(8,128)(2,1)} custom-call(s32[2]{0:T(128)S(1)} %pad_add_fusion.refs_0_, f32[32,128]{1,0:T(8,128)S(1)} %get-tuple-element.31.refs_1_, bf16[8,1792]{1,0:T(8,128)(2,1)S(1)} %get-tuple-element.46.refs_2_, bf16[8,1792]{1,0:T(8,128)(2,1)S(1)} %collective-permute-done.17.refs_3_, ...), custom_call_target="tpu_custom_call" | custom-call | tf_op jit(solution)/shard_map/place_rows/pallas_call | solution.py:282
  (8 shorter events, 0.0 us)
Async XLA Ops:
  0.6 38.1 %copy-start = (bf16[1792,384]{1,0:T(8,128)(2,1)S(1)}, bf16[1792,384]{1,0:T(8,128)(2,1)}, u32[]{:S(2)}) copy-start(bf16[1792,384]{1,0:T(8,128)(2,1)} %gate_ref.1) | copy-start | bytes 4128772
  0.7 1.3 %copy-start.3 = (bf16[128,3584]{1,0:T(8,128)(2,1)S(1)}, bf16[128,3584]{1,0:T(8,128)(2,1)}, u32[]{:S(2)}) copy-start(bf16[128,3584]{1,0:T(8,128)(2,1)} %refs_4_.1) | copy-start | bytes 2752516
  2.0 1.2 %copy-start.4 = (bf16[128,3584]{1,0:T(8,128)(2,1)S(1)}, bf16[128,3584]{1,0:T(8,128)(2,1)}, u32[]{:S(2)}) copy-start(bf16[128,3584]{1,0:T(8,128)(2,1)} %refs_5_.1) | copy-start | bytes 2752516
  3.2 0.7 copy-start.5
  3.9 0.7 copy-start.6
  4.5 0.7 copy-start.7
  6.4 7.1 %collective-permute-start = (bf16[16,1792]{1,0:T(8,128)(2,1)S(1)}, bf16[16,1792]{1,0:T(8,128)(2,1)S(1)}, u32[]{:S(2)}, u32[]{:S(2)}) collective-permute-start(bf16[16,1792]{1,0:T(8,128)(2,1)S(1)} %get-tuple-element.33), channel_id=1, source_target_pairs={{0,1},{1,0},{2,3},{3,2},{4,5},{5,4},{6,7},{7,6},{8,9},{9,8},{10,11... | collective-permute-start | bytes 172040 | tf_op jit(solution)/shard_map/ppermute | solution.py:210
  6.9 8.8 %collective-permute-start.1 = (bf16[16,1792]{1,0:T(8,128)(2,1)S(1)}, bf16[16,1792]{1,0:T(8,128)(2,1)S(1)}, u32[]{:S(2)}, u32[]{:S(2)}) collective-permute-start(bf16[16,1792]{1,0:T(8,128)(2,1)S(1)} %get-tuple-element.34), channel_id=1, source_target_pairs={{0,8},{1,9},{2,10},{3,11},{4,12},{5,13},{6,14},{7,15},{8,16},{9,17... | collective-permute-start | bytes 172040 | tf_op jit(solution)/shard_map/ppermute | solution.py:210
  9.5 6.5 %collective-permute-start.2 = (bf16[16,1792]{1,0:T(8,128)(2,1)S(1)}, bf16[16,1792]{1,0:T(8,128)(2,1)S(1)}, u32[]{:S(2)}, u32[]{:S(2)}) collective-permute-start(bf16[16,1792]{1,0:T(8,128)(2,1)S(1)} %get-tuple-element.35), channel_id=1, source_target_pairs={{0,9},{1,8},{2,11},{3,10},{4,13},{5,12},{6,15},{7,14},{8,17},{9,16... | collective-permute-start | bytes 172040 | tf_op jit(solution)/shard_map/ppermute | solution.py:210
  10.9 8.5 %collective-permute-start.3 = (bf16[16,1792]{1,0:T(8,128)(2,1)S(1)}, bf16[16,1792]{1,0:T(8,128)(2,1)S(1)}, u32[]{:S(2)}, u32[]{:S(2)}) collective-permute-start(bf16[16,1792]{1,0:T(8,128)(2,1)S(1)} %get-tuple-element.36), channel_id=1, source_target_pairs={{0,16},{1,17},{2,18},{3,19},{4,20},{5,21},{6,22},{7,23},{8,24},{9,... | collective-permute-start | bytes 172040 | tf_op jit(solution)/shard_map/ppermute | solution.py:210
  12.2 8.3 %collective-permute-start.4 = (bf16[16,1792]{1,0:T(8,128)(2,1)S(1)}, bf16[16,1792]{1,0:T(8,128)(2,1)S(1)}, u32[]{:S(2)}, u32[]{:S(2)}) collective-permute-start(bf16[16,1792]{1,0:T(8,128)(2,1)S(1)} %get-tuple-element.37), channel_id=1, source_target_pairs={{0,17},{1,16},{2,19},{3,18},{4,21},{5,20},{6,23},{7,22},{8,25},{9,... | collective-permute-start | bytes 172040 | tf_op jit(solution)/shard_map/ppermute | solution.py:210
  13.5 7.0 %collective-permute-start.5 = (bf16[16,1792]{1,0:T(8,128)(2,1)S(1)}, bf16[16,1792]{1,0:T(8,128)(2,1)S(1)}, u32[]{:S(2)}, u32[]{:S(2)}) collective-permute-start(bf16[16,1792]{1,0:T(8,128)(2,1)S(1)} %get-tuple-element.38), channel_id=1, source_target_pairs={{0,24},{1,25},{2,26},{3,27},{4,28},{5,29},{6,30},{7,31},{8,0},{9,1... | collective-permute-start | bytes 172040 | tf_op jit(solution)/shard_map/ppermute | solution.py:210
  15.7 5.9 %collective-permute-start.6 = (bf16[16,1792]{1,0:T(8,128)(2,1)S(1)}, bf16[16,1792]{1,0:T(8,128)(2,1)S(1)}, u32[]{:S(2)}, u32[]{:S(2)}) collective-permute-start(bf16[16,1792]{1,0:T(8,128)(2,1)S(1)} %get-tuple-element.39), channel_id=1, source_target_pairs={{0,25},{1,24},{2,27},{3,26},{4,29},{5,28},{6,31},{7,30},{8,1},{9,0... | collective-permute-start | bytes 172040 | tf_op jit(solution)/shard_map/ppermute | solution.py:210
  22.5 6.6 %collective-permute-start.10 = (bf16[40,1792]{1,0:T(8,128)(2,1)S(1)}, bf16[40,1792]{1,0:T(8,128)(2,1)S(1)}, u32[]{:S(2)}, u32[]{:S(2)}) collective-permute-start(bf16[40,1792]{1,0:T(8,128)(2,1)S(1)} %get-tuple-element.41.refs_4_), channel_id=1, source_target_pairs={{0,2},{2,0},{4,6},{6,4},{8,10},{10,8},{12,14},{14,12},{16,18},{18,... | collective-permute-start | bytes 430088 | tf_op jit(solution)/shard_map/ppermute | solution.py:233
  24.0 9.1 %collective-permute-start.11 = (bf16[40,1792]{1,0:T(8,128)(2,1)S(1)}, bf16[40,1792]{1,0:T(8,128)(2,1)S(1)}, u32[]{:S(2)}, u32[]{:S(2)}) collective-permute-start(bf16[40,1792]{1,0:T(8,128)(2,1)S(1)} %get-tuple-element.41.refs_4_), channel_id=1, source_target_pairs={{0,4},{2,6},{4,0},{6,2},{8,12},{10,14},{12,8},{14,10},{16,20},{18,... | collective-permute-start | bytes 430088 | tf_op jit(solution)/shard_map/ppermute | solution.py:233
  25.5 7.6 %collective-permute-start.12 = (bf16[40,1792]{1,0:T(8,128)(2,1)S(1)}, bf16[40,1792]{1,0:T(8,128)(2,1)S(1)}, u32[]{:S(2)}, u32[]{:S(2)}) collective-permute-start(bf16[40,1792]{1,0:T(8,128)(2,1)S(1)} %get-tuple-element.41.refs_4_), channel_id=1, source_target_pairs={{0,6},{2,4},{4,2},{6,0},{8,14},{10,12},{12,10},{14,8},{16,22},{18,... | collective-permute-start | bytes 430088 | tf_op jit(solution)/shard_map/ppermute | solution.py:233
  26.0 9.3 %collective-permute-start.7 = (bf16[40,1792]{1,0:T(8,128)(2,1)S(1)}, bf16[40,1792]{1,0:T(8,128)(2,1)S(1)}, u32[]{:S(2)}, u32[]{:S(2)}) collective-permute-start(bf16[40,1792]{1,0:T(8,128)(2,1)S(1)} %get-tuple-element.40.refs_0_), channel_id=1, source_target_pairs={{0,2},{2,0},{4,6},{6,4},{8,10},{10,8},{12,14},{14,12},{16,18},{18,... | collective-permute-start | bytes 430088 | tf_op jit(solution)/shard_map/ppermute | solution.py:232
  27.5 11.2 %collective-permute-start.8 = (bf16[40,1792]{1,0:T(8,128)(2,1)S(1)}, bf16[40,1792]{1,0:T(8,128)(2,1)S(1)}, u32[]{:S(2)}, u32[]{:S(2)}) collective-permute-start(bf16[40,1792]{1,0:T(8,128)(2,1)S(1)} %get-tuple-element.40.refs_0_), channel_id=1, source_target_pairs={{0,4},{2,6},{4,0},{6,2},{8,12},{10,14},{12,8},{14,10},{16,20},{18,... | collective-permute-start | bytes 430088 | tf_op jit(solution)/shard_map/ppermute | solution.py:232
  29.0 9.7 %collective-permute-start.9 = (bf16[40,1792]{1,0:T(8,128)(2,1)S(1)}, bf16[40,1792]{1,0:T(8,128)(2,1)S(1)}, u32[]{:S(2)}, u32[]{:S(2)}) collective-permute-start(bf16[40,1792]{1,0:T(8,128)(2,1)S(1)} %get-tuple-element.40.refs_0_), channel_id=1, source_target_pairs={{0,6},{2,4},{4,2},{6,0},{8,14},{10,12},{12,10},{14,8},{16,22},{18,... | collective-permute-start | bytes 430088 | tf_op jit(solution)/shard_map/ppermute | solution.py:232
  38.7 1.3 %copy-start.1 = (bf16[1792,384]{1,0:T(8,128)(2,1)S(1)}, bf16[1792,384]{1,0:T(8,128)(2,1)}, u32[]{:S(2)}) copy-start(bf16[1792,384]{1,0:T(8,128)(2,1)} %up_ref.1) | copy-start | bytes 4128772
  40.1 1.3 %copy-start.2 = (bf16[1792,384]{1,0:T(8,128)(2,1)S(1)}, bf16[1792,384]{1,0:T(8,128)(2,1)}, u32[]{:S(2)}) copy-start(bf16[1792,384]{1,0:T(8,128)(2,1)} %refs_10_.1) | copy-start | bytes 4128772
  44.2 2.3 %collective-permute-start.13 = (f32[160,1152]{1,0:T(8,128)S(1)}, f32[160,1152]{1,0:T(8,128)S(1)}, u32[]{:S(2)}, u32[]{:S(2)}) collective-permute-start(f32[160,1152]{1,0:T(8,128)S(1)} %partial_products.1.mine_ref), channel_id=1, source_target_pairs={{0,1},{1,0},{2,3},{3,2},{4,5},{5,4},{6,7},{7,6},{8,9},{9,8},{10,11... | collective-permute-start | bytes 2211848 | tf_op jit(solution)/shard_map/ppermute | solution.py:250
  48.7 6.7 %collective-permute-start.14 = (bf16[40,1792]{1,0:T(8,128)(2,1)S(1)}, bf16[40,1792]{1,0:T(8,128)(2,1)S(1)}, u32[]{:S(2)}, u32[]{:S(2)}) collective-permute-start(bf16[40,1792]{1,0:T(8,128)(2,1)S(1)} %get-tuple-element.43), channel_id=1, source_target_pairs={{0,2},{2,0},{4,6},{6,4},{8,10},{10,8},{12,14},{14,12},{16,18},{18,... | collective-permute-start | bytes 430088 | tf_op jit(solution)/shard_map/ppermute | solution.py:262
  50.0 7.0 %collective-permute-start.15 = (bf16[40,1792]{1,0:T(8,128)(2,1)S(1)}, bf16[40,1792]{1,0:T(8,128)(2,1)S(1)}, u32[]{:S(2)}, u32[]{:S(2)}) collective-permute-start(bf16[40,1792]{1,0:T(8,128)(2,1)S(1)} %get-tuple-element.44), channel_id=1, source_target_pairs={{0,4},{2,6},{4,0},{6,2},{8,12},{10,14},{12,8},{14,10},{16,20},{18,... | collective-permute-start | bytes 430088 | tf_op jit(solution)/shard_map/ppermute | solution.py:262
  50.8 7.8 %collective-permute-start.16 = (bf16[40,1792]{1,0:T(8,128)(2,1)S(1)}, bf16[40,1792]{1,0:T(8,128)(2,1)S(1)}, u32[]{:S(2)}, u32[]{:S(2)}) collective-permute-start(bf16[40,1792]{1,0:T(8,128)(2,1)S(1)} %get-tuple-element.45), channel_id=1, source_target_pairs={{0,6},{2,4},{4,2},{6,0},{8,14},{10,12},{12,10},{14,8},{16,22},{18,... | collective-permute-start | bytes 430088 | tf_op jit(solution)/shard_map/ppermute | solution.py:262
  59.4 5.3 %collective-permute-start.17 = (bf16[8,1792]{1,0:T(8,128)(2,1)S(1)}, bf16[8,1792]{1,0:T(8,128)(2,1)S(1)}, u32[]{:S(2)}, u32[]{:S(2)}) collective-permute-start(bf16[8,1792]{1,0:T(8,128)(2,1)S(1)} %get-tuple-element.47), channel_id=1, source_target_pairs={{1,0},{0,1},{3,2},{2,3},{5,4},{4,5},{7,6},{6,7},{9,8},{8,9},{11,10... | collective-permute-start | bytes 86024 | tf_op jit(solution)/shard_map/ppermute | solution.py:210
  59.5 7.1 %collective-permute-start.18 = (bf16[8,1792]{1,0:T(8,128)(2,1)S(1)}, bf16[8,1792]{1,0:T(8,128)(2,1)S(1)}, u32[]{:S(2)}, u32[]{:S(2)}) collective-permute-start(bf16[8,1792]{1,0:T(8,128)(2,1)S(1)} %get-tuple-element.48), channel_id=1, source_target_pairs={{8,0},{9,1},{10,2},{11,3},{12,4},{13,5},{14,6},{15,7},{16,8},{17,9... | collective-permute-start | bytes 86024 | tf_op jit(solution)/shard_map/ppermute | solution.py:210
  62.2 9.2 %collective-permute-start.19 = (bf16[8,1792]{1,0:T(8,128)(2,1)S(1)}, bf16[8,1792]{1,0:T(8,128)(2,1)S(1)}, u32[]{:S(2)}, u32[]{:S(2)}) collective-permute-start(bf16[8,1792]{1,0:T(8,128)(2,1)S(1)} %get-tuple-element.49), channel_id=1, source_target_pairs={{9,0},{8,1},{11,2},{10,3},{13,4},{12,5},{15,6},{14,7},{17,8},{16,9... | collective-permute-start | bytes 86024 | tf_op jit(solution)/shard_map/ppermute | solution.py:210
  62.3 9.1 %collective-permute-start.20 = (bf16[8,1792]{1,0:T(8,128)(2,1)S(1)}, bf16[8,1792]{1,0:T(8,128)(2,1)S(1)}, u32[]{:S(2)}, u32[]{:S(2)}) collective-permute-start(bf16[8,1792]{1,0:T(8,128)(2,1)S(1)} %get-tuple-element.50), channel_id=1, source_target_pairs={{16,0},{17,1},{18,2},{19,3},{20,4},{21,5},{22,6},{23,7},{24,8},{25... | collective-permute-start | bytes 86024 | tf_op jit(solution)/shard_map/ppermute | solution.py:210
  62.8 8.5 %collective-permute-start.21 = (bf16[8,1792]{1,0:T(8,128)(2,1)S(1)}, bf16[8,1792]{1,0:T(8,128)(2,1)S(1)}, u32[]{:S(2)}, u32[]{:S(2)}) collective-permute-start(bf16[8,1792]{1,0:T(8,128)(2,1)S(1)} %get-tuple-element.51), channel_id=1, source_target_pairs={{17,0},{16,1},{19,2},{18,3},{21,4},{20,5},{23,6},{22,7},{25,8},{24... | collective-permute-start | bytes 86024 | tf_op jit(solution)/shard_map/ppermute | solution.py:210
  64.7 6.7 %collective-permute-start.22 = (bf16[8,1792]{1,0:T(8,128)(2,1)S(1)}, bf16[8,1792]{1,0:T(8,128)(2,1)S(1)}, u32[]{:S(2)}, u32[]{:S(2)}) collective-permute-start(bf16[8,1792]{1,0:T(8,128)(2,1)S(1)} %get-tuple-element.52), channel_id=1, source_target_pairs={{24,0},{25,1},{26,2},{27,3},{28,4},{29,5},{30,6},{31,7},{0,8},{1,9... | collective-permute-start | bytes 86024 | tf_op jit(solution)/shard_map/ppermute | solution.py:210
  66.6 5.1 %collective-permute-start.23 = (bf16[8,1792]{1,0:T(8,128)(2,1)S(1)}, bf16[8,1792]{1,0:T(8,128)(2,1)S(1)}, u32[]{:S(2)}, u32[]{:S(2)}) collective-permute-start(bf16[8,1792]{1,0:T(8,128)(2,1)S(1)} %get-tuple-element.53), channel_id=1, source_target_pairs={{25,0},{24,1},{27,2},{26,3},{29,4},{28,5},{31,6},{30,7},{1,8},{0,9... | collective-permute-start | bytes 86024 | tf_op jit(solution)/shard_map/ppermute | solution.py:210
